TPU v7x, 256 devices: a whole 4x4x8 slice. The times are simulated.
256 devices in a mesh: row: 8 (over z_lo, y), col: 4 (over z_hi), depth: 8 (over x, core).
Axes of the slice: x: 4, y: 4, z: 8 (z_hi: 4, z_lo: 2; z = z_hi * 2 + z_lo), core: 2. Of those that a mesh axis runs over, the one named last changes fastest.
Arguments:
- tokens: bfloat16 [2048, 12288], P(('row', 'col'), 'depth'), may hold values from -6 to 6
- weight: bfloat16 [12288, 24576], P('depth', ('row', 'col')), may hold values from -5 to 5
- moment: bfloat16 [12288, 24576], P('depth', ('row', 'col')), may hold values from -0.59765625 to 0.59765625
- upstream: bfloat16 [8, 256, 24576], P(None, 'col', ('row', 'depth')), may hold values from -24 to 24
Outputs:
- activated: bfloat16 [8, 256, 24576], P(None, 'col', ('row', 'depth'))
- new_weight: bfloat16 [12288, 24576], P('depth', ('row', 'col'))
- new_moment: bfloat16 [12288, 24576], P('depth', ('row', 'col'))
All inputs are finite; a program needn't handle non-finite values.
Results may differ from a plain program's by a relative error of at most 0.015.
Values may be sent and summed in bfloat16 or wider, within the bound.
A program may use at most 64 MiB of HBM per device.

v0:
```python
import jax
import jax.numpy as jnp
from jax import lax
from jax.sharding import PartitionSpec as P

D = 12288
gelu_coef = 0.7978845608028654
cubic_coef = 0.044715
lion_rate = 0.5
decay_rate = 0.1
beta_one = 0.9
beta_two = 0.99
smooth_tau = 0.1


def gelu_pair(preact):
    tangent = jnp.tanh(gelu_coef * (preact + cubic_coef * preact * preact * preact))
    gelu_value = 0.5 * preact * (1.0 + tangent)
    gelu_slope = 0.5 * (1.0 + tangent) + 0.5 * preact * (1.0 - tangent * tangent) * gelu_coef * (
        1.0 + 3.0 * cubic_coef * preact * preact
    )
    return (gelu_value, gelu_slope)


def shards(tokens, weight, moment, upstream):
    row_count = lax.axis_size("row")
    tok_rows = tokens.shape[0]
    fan_scale = D ** (-0.5)
    gathered = lax.all_gather(tokens, "row", axis=0, tiled=True)
    partial_value = jnp.dot(
        gathered,
        lax.all_gather(weight, "col", axis=1, tiled=True),
        preferred_element_type=jnp.float32,
    )
    summed = lax.psum_scatter(
        partial_value.astype(jnp.bfloat16), "depth", scatter_dimension=1, tiled=True
    ).astype(jnp.float32)
    gelu_value, gelu_slope = gelu_pair(summed * fan_scale)
    activated = gelu_value.astype(jnp.bfloat16)
    upstream_flat = upstream.reshape(row_count * tok_rows, upstream.shape[2]).astype(jnp.float32)
    local_grad = (upstream_flat * gelu_slope).astype(jnp.bfloat16)
    act_grad = lax.all_gather(local_grad, "depth", axis=1, tiled=True)
    grad_panel = lax.dot_general(
        gathered, act_grad, (((0,), (0,)), ((), ())), preferred_element_type=jnp.float32
    )
    grad_sum = lax.psum_scatter(
        grad_panel.astype(jnp.bfloat16), "col", scatter_dimension=1, tiled=True
    ).astype(jnp.float32)
    grad_full = grad_sum * fan_scale
    moment_f = moment.astype(jnp.float32)
    weight_f = weight.astype(jnp.float32)
    blended = beta_one * moment_f + (1.0 - beta_one) * grad_full
    update = blended / jnp.sqrt(blended * blended + smooth_tau * smooth_tau)
    new_weight = (weight_f - lion_rate * (update + decay_rate * weight_f)).astype(jnp.bfloat16)
    new_moment = (beta_two * moment_f + (1.0 - beta_two) * grad_full).astype(jnp.bfloat16)
    activated = activated.reshape(upstream.shape[0], upstream.shape[1], activated.shape[1])
    return (activated, new_weight, new_moment)


def solution(mesh):
    placed = (
        P(("row", "col"), "depth"),
        P("depth", ("row", "col")),
        P("depth", ("row", "col")),
        P(None, "col", ("row", "depth")),
    )
    return jax.shard_map(
        shards,
        mesh=mesh,
        in_specs=placed,
        out_specs=(
            P(None, "col", ("row", "depth")),
            P("depth", ("row", "col")),
            P("depth", ("row", "col")),
        ),
        check_vma=False,
    )
```

profile of v0, /device:TPU:2, one launch (start us, length us, event | category | flops | bytes accessed | tf_op | source)
XLA Modules:
  0.0 509.9 jit_solution(10022676626198729526)
XLA Ops:
  7.2 0.0 all-gather.4.cloned.1.call-start
  7.2 0.7 all-gather.4.cloned.1.call-update
  7.9 0.0 all-gather.6.cloned.1.call-start
  7.9 0.7 all-gather.6.cloned.1.call-update
  8.6 0.0 reduce-scatter.7.cloned.1.call-start
  8.7 47.2 %all-gather.4.cloned.1.call-done = bf16[512,1536]{1,0:T(8,128)(2,1)} async-done(((bf16[64,1536]{1,0:T(8,128)(2,1)}), bf16[512,1536]{1,0:T(8,128)(2,1)}) %all-gather.4.cloned.1.call-update) | async-done | bytes 1572880 | tf_op jit(solution)/shard_map/all_gather | solution.py:29
  55.9 173.9 %all-gather.6.cloned.1.call-done = bf16[1536,3072]{1,0:T(8,128)(2,1)} async-done(((bf16[1536,768]{1,0:T(8,128)(2,1)}), bf16[1536,3072]{1,0:T(8,128)(2,1)}) %all-gather.6.cloned.1.call-update) | async-done | bytes 9437200 | tf_op jit(solution)/shard_map/all_gather | solution.py:32
  229.8 8.1 %convolution_convert_fusion.1 = bf16[512,3072]{1,0:T(8,128)(2,1)S(1)} fusion(bf16[512,1536]{1,0:T(8,128)(2,1)} %all-gather.4.cloned.1.call-done, bf16[1536,3072]{1,0:T(8,128)(2,1)} %all-gather.6.cloned.1.call-done), kind=kOutput, calls=%fused_computation.14 | convolution fusion | flops 4833411072 | bytes 14155776 | tf_op jit(solution)/shard_map/dot_general | solution.py:30
  237.9 2.8 copy.15
  240.8 0.0 all-gather.8.cloned.1.call-start
  240.8 33.4 %reduce-scatter.7.cloned.1.call-done = bf16[384,512]{1,0:T(8,128)(2,1)} async-done(((bf16[3072,512]{1,0:T(8,128)(2,1)}), bf16[384,512]{1,0:T(8,128)(2,1)}) %reduce-scatter.7.cloned.1.call-update) | async-done | bytes 393232
  274.2 1.2 copy.16
  275.4 1.5 fusion.18
  277.0 0.0 all-gather.8.cloned.1.call-update
  277.0 0.0 reduce-scatter.5.cloned.1.call-start
  277.0 31.8 %all-gather.8.cloned.1.call-done = bf16[512,3072]{1,0:T(8,128)(2,1)} async-done(((bf16[512,384]{1,0:T(8,128)(2,1)}), bf16[512,3072]{1,0:T(8,128)(2,1)}) %all-gather.8.cloned.1.call-update) | async-done | bytes 3145744 | tf_op jit(solution)/shard_map/all_gather | solution.py:42
  308.8 9.6 %fusion = bf16[1536,3072]{0,1:T(8,128)(2,1)} fusion(bf16[512,3072]{1,0:T(8,128)(2,1)} %all-gather.8.cloned.1.call-done, bf16[512,1536]{1,0:T(8,128)(2,1)S(1)} %copy-done.4), kind=kOutput, calls=%fused_computation.1 | convolution fusion | flops 4836556800 | bytes 14155776 | tf_op jit(solution)/shard_map/dot_general | solution.py:43
  318.4 1.6 copy-done
  320.1 2.4 copy.11
  322.5 4.4 copy.12
  326.9 163.8 %reduce-scatter.5.cloned.1.call-done = bf16[1536,768]{0,1:T(8,128)(2,1)} async-done(((bf16[1536,3072]{0,1:T(8,128)(2,1)}), bf16[1536,768]{0,1:T(8,128)(2,1)}) %reduce-scatter.5.cloned.1.call-update) | async-done | bytes 2359312 | tf_op jit(solution)/shard_map/reduce_scatter | solution.py:46
  490.7 5.9 %fusion.6 = (bf16[1536,768]{0,1:T(8,128)(2,1)}, bf16[1536,768]{0,1:T(8,128)(2,1)}) fusion(bf16[1536,768]{0,1:T(8,128)(2,1)} %copy.12, bf16[1536,768]{0,1:T(8,128)(2,1)} %reduce-scatter.5.cloned.1.call-done, bf16[1536,768]{0,1:T(8,128)(2,1)S(1)} %copy-done.1), kind=kLoop, calls=%fused_computation.13 | loop fusion | flops 21233664 | bytes 11796480 | tf_op jit(solution)/shard_map/convert_element_type | solution.py:55
  496.6 4.4 copy.13
  501.0 2.4 copy.14
  (11 shorter events, 0.1 us)
Async XLA Ops:
  7.2 48.8 %all-gather.4.cloned.1.call-start = ((), (), s32[]{:S(2)}) async-start(), calls=%async_computation.2 | async-start | bytes 1769472 | tf_op jit(solution)/shard_map/all_gather | solution.py:29
  7.9 221.9 %all-gather.6.cloned.1.call-start = ((), (), s32[]{:S(2)}) async-start(), calls=%async_computation.3 | async-start | bytes 11796480 | tf_op jit(solution)/shard_map/all_gather | solution.py:32
  8.6 265.6 %reduce-scatter.7.cloned.1.call-start = ((), (), s32[]{:S(2)}) async-start(), calls=%async_computation.6 | async-start | bytes 3538944
  237.9 37.5 %copy-start.3 = (bf16[8,64,384]{2,1,0:T(8,128)(2,1)S(1)}, bf16[8,64,384]{2,1,0:T(8,128)(2,1)}, u32[]{:S(2)}) copy-start(bf16[8,64,384]{2,1,0:T(8,128)(2,1)} %param.7) | copy-start | bytes 1179652
  240.7 68.1 %copy-start.4 = (bf16[512,1536]{1,0:T(8,128)(2,1)S(1)}, bf16[512,1536]{1,0:T(8,128)(2,1)}, u32[]{:S(2)}) copy-start(bf16[512,1536]{1,0:T(8,128)(2,1)} %all-gather.4.cloned.1.call-done) | copy-start | bytes 4718596
  240.8 68.0 %all-gather.8.cloned.1.call-start = ((), (), s32[]{:S(2)}) async-start(), calls=%async_computation.4 | async-start | bytes 3538944 | tf_op jit(solution)/shard_map/all_gather | solution.py:42
  277.0 213.7 %reduce-scatter.5.cloned.1.call-start = ((), (), s32[]{:S(2)}) async-start(), calls=%async_computation.5 | async-start | bytes 11796480 | tf_op jit(solution)/shard_map/reduce_scatter | solution.py:46
  318.4 1.7 copy-start
  322.5 168.2 %copy-start.1 = (bf16[1536,768]{0,1:T(8,128)(2,1)S(1)}, bf16[1536,768]{0,1:T(8,128)(2,1)}, u32[]{:S(2)}) copy-start(bf16[1536,768]{0,1:T(8,128)(2,1)} %copy.11) | copy-start | bytes 7077892
  496.6 4.4 copy-start.2
Sparse Core Ops, SparseCore 0:
  9.8 46.0 all-gather.3
  57.7 172.0 all-gather.5
  240.9 33.2 reduce-scatter.6
  277.1 31.6 all-gather.7
  318.5 172.1 reduce-scatter.4
where the time goes:
time: 510 us
  waiting for transfers between devices  452 us (89%)
  local copies, waits for them, and re-layouts  19.4 us (4%)
  matrix products  17.7 us (3%)
  between operations  13.8 us (3%)
  other arithmetic  7.4 us (1%)
    all_gather x1, waiting for transfers between devices, shards(): lax.all_gather(weight, 'col', axis=1, tiled=True)  174 us
    reduce_scatter x1, waiting for transfers between devices, shards(): lax.psum_scatter(grad_panel.astype(jnp.bfloat16), 'col', scatter_dimensio...  164 us
    all_gather x1, waiting for transfers between devices, shards(): gathered = lax.all_gather(tokens, 'row', axis=0, tiled=True)  47.2 us
    unnamed x6, waiting for transfers between devices  34.8 us
    all_gather x1, waiting for transfers between devices, shards(): act_grad = lax.all_gather(local_grad, 'depth', axis=1, tiled=True)  31.8 us
    unnamed x16, local copies, waits for them, and re-layouts  19.4 us
  transfers between devices with their start and end apart: 5, of which 5 were waited for; matrix products, arithmetic and copies ran while one was open for 1% of the time, Pallas kernels for 0%

commit v1 on v0

--- a/solution.py
+++ b/solution.py
@@ -11,6 +11,25 @@
 beta_one = 0.9
 beta_two = 0.99
 smooth_tau = 0.1
+
+
+def laid_out(tiles, dim):
+    shape = list(tiles.shape[1:])
+    shape[dim] *= tiles.shape[0]
+    return jnp.moveaxis(tiles, 0, dim).reshape(shape)
+
+
+def grow_blocks(value, axis):
+    count, index = (lax.axis_size(axis), lax.axis_index(axis))
+    tiles, stride = (value[None], 1)
+    while stride < count:
+        partner_block = lax.ppermute(tiles, axis, [(i, i ^ stride) for i in range(count)])
+        low = index & stride == 0
+        tiles = jnp.concatenate(
+            [jnp.where(low, tiles, partner_block), jnp.where(low, partner_block, tiles)]
+        )
+        stride *= 2
+    return tiles
 
 
 def gelu_pair(preact):
@@ -39,7 +58,7 @@
     activated = gelu_value.astype(jnp.bfloat16)
     upstream_flat = upstream.reshape(row_count * tok_rows, upstream.shape[2]).astype(jnp.float32)
     local_grad = (upstream_flat * gelu_slope).astype(jnp.bfloat16)
-    act_grad = lax.all_gather(local_grad, "depth", axis=1, tiled=True)
+    act_grad = laid_out(grow_blocks(local_grad, "depth"), 1)
     grad_panel = lax.dot_general(
         gathered, act_grad, (((0,), (0,)), ((), ())), preferred_element_type=jnp.float32
     )

time: 510 us -> 544 us (1.067)
  waiting for transfers between devices: 452 us -> 473 us
  starting transfers between devices: 0.2 us -> 5.81 us
    ppermute x0 -> x3, waiting for transfers between devices: none -> 55.6 us  [grow_blocks(): lax.ppermute(tiles, axis, [(i, i ^ stride) for i in range(count)])]
    all_gather x1 -> x0, waiting for transfers between devices: 31.8 us -> none  [shards(): act_grad = lax.all_gather(local_grad, 'depth', axis=1, tiled=True)]
    ppermute x0 -> x3, starting transfers between devices: none -> 5.66 us  [grow_blocks(): lax.ppermute(tiles, axis, [(i, i ^ stride) for i in range(count)])]
    unnamed x6 -> x5, waiting for transfers between devices: 34.8 us -> 34.8 us
    unnamed x16 -> x14, local copies, waits for them, and re-layouts: 19.4 us -> 19.4 us
  transfers between devices with their start and end apart: 5 -> 7, of which waited for: 5 -> 7; matrix products, arithmetic and copies ran while one was open for 1% -> 1% of each run, Pallas kernels for 0% -> 0%
where the time goes in v1:
time: 544 us; the launch traced here: 542 us
  waiting for transfers between devices  473 us (87%)
  local copies, waits for them, and re-layouts  22.2 us (4%)
  matrix products  17.4 us (3%)
  between operations  13.8 us (3%)
  other arithmetic  9.97 us (2%)
  starting transfers between devices  5.81 us (1%)
    all_gather x1, waiting for transfers between devices, shards(): lax.all_gather(weight, 'col', axis=1, tiled=True)  174 us
    reduce_scatter x1, waiting for transfers between devices, shards(): lax.psum_scatter(grad_panel.astype(jnp.bfloat16), 'col', scatter_dimensio...  161 us
    ppermute x3, waiting for transfers between devices, grow_blocks(): lax.ppermute(tiles, axis, [(i, i ^ stride) for i in range(count)])  55.6 us
    all_gather x1, waiting for transfers between devices, shards(): gathered = lax.all_gather(tokens, 'row', axis=0, tiled=True)  47.2 us
    unnamed x5, waiting for transfers between devices  34.8 us
    unnamed x14, local copies, waits for them, and re-layouts  19.4 us
  transfers between devices with their start and end apart: 7, of which 7 were waited for; matrix products, arithmetic and copies ran while one was open for 1% of the time, Pallas kernels for 0%

profile of v1, /device:TPU:2, one launch (start us, length us, event | category | flops | bytes accessed | tf_op | source)
XLA Modules:
  0.0 542.1 jit_solution(12554795887554093073)
XLA Ops:
  7.2 0.7 all-gather.3.cloned.1.call-update
  7.9 0.7 all-gather.5.cloned.1.call-update
  8.7 47.2 %all-gather.3.cloned.1.call-done = bf16[512,1536]{1,0:T(8,128)(2,1)} async-done(((bf16[64,1536]{1,0:T(8,128)(2,1)}), bf16[512,1536]{1,0:T(8,128)(2,1)}) %all-gather.3.cloned.1.call-update) | async-done | bytes 1572880 | tf_op jit(solution)/shard_map/all_gather | solution.py:48
  55.9 173.9 %all-gather.5.cloned.1.call-done = bf16[1536,3072]{1,0:T(8,128)(2,1)} async-done(((bf16[1536,768]{1,0:T(8,128)(2,1)}), bf16[1536,3072]{1,0:T(8,128)(2,1)}) %all-gather.5.cloned.1.call-update) | async-done | bytes 9437200 | tf_op jit(solution)/shard_map/all_gather | solution.py:51
  229.8 8.1 %convolution_convert_fusion.1 = bf16[512,3072]{1,0:T(8,128)(2,1)S(1)} fusion(bf16[512,1536]{1,0:T(8,128)(2,1)} %all-gather.3.cloned.1.call-done, bf16[1536,3072]{1,0:T(8,128)(2,1)} %all-gather.5.cloned.1.call-done), kind=kOutput, calls=%fused_computation.14 | convolution fusion | flops 4833411072 | bytes 14155776 | tf_op jit(solution)/shard_map/dot_general | solution.py:49
  237.9 2.8 copy.28
  240.8 33.4 %reduce-scatter.7.cloned.1.call-done = bf16[384,512]{1,0:T(8,128)(2,1)} async-done(((bf16[3072,512]{1,0:T(8,128)(2,1)}), bf16[384,512]{1,0:T(8,128)(2,1)}) %reduce-scatter.7.cloned.1.call-update) | async-done | bytes 393232
  274.2 1.2 copy.29
  275.4 1.4 fusion.18
  276.8 1.7 collective-permute-done
  278.7 4.0 collective-permute-start.1
  282.8 17.8 %collective-permute-done.1 = bf16[2,512,384]{2,1,0:T(8,128)(2,1)S(1)} collective-permute-done((bf16[2,512,384]{2,1,0:T(8,128)(2,1)S(1)}, bf16[2,512,384]{2,1,0:T(8,128)(2,1)S(1)}, u32[]{:S(2)}, u32[]{:S(2)}) %collective-permute-start.1) | collective-permute-done | bytes 786464 | tf_op jit(solution)/shard_map/ppermute | solution.py:26
  301.0 1.6 collective-permute-start.2
  302.6 36.0 %collective-permute-done.2 = bf16[4,512,384]{2,1,0:T(8,128)(2,1)} collective-permute-done((bf16[4,512,384]{2,1,0:T(8,128)(2,1)S(1)}, bf16[4,512,384]{2,1,0:T(8,128)(2,1)}, u32[]{:S(2)}, u32[]{:S(2)}) %collective-permute-start.2) | collective-permute-done | bytes 1572896 | tf_op jit(solution)/shard_map/ppermute | solution.py:26
  338.6 1.8 broadcast_select_fusion.1
  340.8 2.9 copy.25
  343.7 9.3 %fusion = bf16[1536,3072]{0,1:T(8,128)(2,1)} fusion(bf16[512,3072]{0,1:T(8,128)(2,1)} %bitcast.19, bf16[512,1536]{1,0:T(8,128)(2,1)} %all-gather.3.cloned.1.call-done), kind=kOutput, calls=%fused_computation.1 | convolution fusion | flops 4836556800 | bytes 14155776 | tf_op jit(solution)/shard_map/dot_general | solution.py:62
  353.0 1.6 copy-done
  354.6 2.4 copy.23
  357.1 4.4 copy.24
  361.5 161.4 %reduce-scatter.5.cloned.1.call-done = bf16[1536,768]{0,1:T(8,128)(2,1)} async-done(((bf16[1536,3072]{0,1:T(8,128)(2,1)}), bf16[1536,768]{0,1:T(8,128)(2,1)}) %reduce-scatter.5.cloned.1.call-update) | async-done | bytes 2359312 | tf_op jit(solution)/shard_map/reduce_scatter | solution.py:65
  522.9 5.8 %fusion.6 = (bf16[1536,768]{0,1:T(8,128)(2,1)}, bf16[1536,768]{0,1:T(8,128)(2,1)}) fusion(bf16[1536,768]{0,1:T(8,128)(2,1)} %copy.24, bf16[1536,768]{0,1:T(8,128)(2,1)} %reduce-scatter.5.cloned.1.call-done, bf16[1536,768]{0,1:T(8,128)(2,1)S(1)} %copy-done.1), kind=kLoop, calls=%fused_computation.13 | loop fusion | flops 21233664 | bytes 11796480 | tf_op jit(solution)/shard_map/convert_element_type | solution.py:74
  528.7 4.4 copy.26
  533.2 2.4 copy.27
  (19 shorter events, 1.1 us)
Async XLA Ops:
  7.2 48.8 %all-gather.3.cloned.1.call-start = ((), (), s32[]{:S(2)}) async-start(), calls=%async_computation.2 | async-start | bytes 1769472 | tf_op jit(solution)/shard_map/all_gather | solution.py:48
  7.9 221.9 %all-gather.5.cloned.1.call-start = ((), (), s32[]{:S(2)}) async-start(), calls=%async_computation.3 | async-start | bytes 11796480 | tf_op jit(solution)/shard_map/all_gather | solution.py:51
  8.6 265.6 %reduce-scatter.7.cloned.1.call-start = ((), (), s32[]{:S(2)}) async-start(), calls=%async_computation.5 | async-start | bytes 3538944
  240.7 34.7 %copy-start.3 = (bf16[8,64,384]{2,1,0:T(8,128)(2,1)S(1)}, bf16[8,64,384]{2,1,0:T(8,128)(2,1)}, u32[]{:S(2)}) copy-start(bf16[8,64,384]{2,1,0:T(8,128)(2,1)} %param.7) | copy-start | bytes 1179652
  240.8 282.1 %reduce-scatter.5.cloned.1.call-start = ((), (), s32[]{:S(2)}) async-start(), calls=%async_computation.4 | async-start | bytes 11796480 | tf_op jit(solution)/shard_map/reduce_scatter | solution.py:65
  276.8 1.7 collective-permute-start
  278.7 21.9 %collective-permute-start.1 = (bf16[2,512,384]{2,1,0:T(8,128)(2,1)S(1)}, bf16[2,512,384]{2,1,0:T(8,128)(2,1)S(1)}, u32[]{:S(2)}, u32[]{:S(2)}) collective-permute-start(bf16[2,512,384]{2,1,0:T(8,128)(2,1)S(1)} %pad_maximum_fusion.1), channel_id=1, source_target_pairs={{0,2},{1,3},{2,0},{3,1},{4,6},{5,7},{6,4},{7,5},{8,10},{9,11},{10,... | collective-permute-start | bytes 2359304 | tf_op jit(solution)/shard_map/ppermute | solution.py:26
  301.0 37.6 %collective-permute-start.2 = (bf16[4,512,384]{2,1,0:T(8,128)(2,1)S(1)}, bf16[4,512,384]{2,1,0:T(8,128)(2,1)}, u32[]{:S(2)}, u32[]{:S(2)}) collective-permute-start(bf16[4,512,384]{2,1,0:T(8,128)(2,1)S(1)} %pad_maximum_fusion), channel_id=1, source_target_pairs={{0,4},{1,5},{2,6},{3,7},{4,0},{5,1},{6,2},{7,3},{8,12},{9,13},{10,... | collective-permute-start | bytes 4718600 | tf_op jit(solution)/shard_map/ppermute | solution.py:26
  353.0 1.7 copy-start
  357.1 165.8 %copy-start.1 = (bf16[1536,768]{0,1:T(8,128)(2,1)S(1)}, bf16[1536,768]{0,1:T(8,128)(2,1)}, u32[]{:S(2)}) copy-start(bf16[1536,768]{0,1:T(8,128)(2,1)} %copy.23) | copy-start | bytes 7077892
  528.7 4.4 copy-start.2
Sparse Core Ops, SparseCore 0:
  9.8 46.0 all-gather.2
  57.7 172.0 all-gather.4
  240.9 33.2 reduce-scatter.6
  353.1 169.7 reduce-scatter.4
